TPU v7x, 512 devices: a whole 4x4x16 slice. The times are simulated.
512 devices in a mesh: seq: 64 (over y, z), head: 8 (over x, core).
Axes of the slice: x: 4, y: 4, z: 16, core: 2. Of those that a mesh axis runs over, the one named last changes fastest.
Arguments:
- queries: bfloat16 [1024, 4096], P('seq', 'head'), may hold values from -9 to 9
- keys: bfloat16 [8, 131072, 128], P('head', 'seq'), may hold values from -9 to 9
- values: bfloat16 [8, 131072, 128], P('head', 'seq'), may hold values from -6 to 6
- mask: int32 [8, 1024], P(None, 'seq'), may hold values from 0 to 1, as said below
- out_proj: bfloat16 [4096, 4096], P('head', 'seq'), may hold values from -0.09375 to 0.09375
Outputs:
- output: bfloat16 [1024, 4096], P('seq', 'head')
Inputs may be any that keep to these rules, and one draw needn't show every extreme that they name: `mask`: each entry is 0 or 1; the share of ones differs strongly between the cached positions of different seq shards.
All inputs are finite; a program needn't handle non-finite values.
Results may differ from a plain program's by a relative error of at most 0.0057.
Values may be sent and summed in bfloat16 or wider, within the bound.
A program may use at most 64 MiB of HBM per device.

v0:
```python
import jax
import jax.numpy as jnp
from jax import lax
from jax.sharding import PartitionSpec as P

BLK = 128


def on_device(queries, keys, values, mask, out_proj):
    gathered = lax.all_gather(queries, "seq", axis=0, tiled=True)
    rows = gathered.shape[0]
    head_size = keys.shape[2]
    group = gathered.shape[1] // head_size
    cached = keys.shape[1]
    query_heads = gathered.reshape(rows, group, head_size)
    key_local = keys[0]
    value_local = values[0]
    block = min(512, cached)
    count = cached // block
    mask_cols = block // BLK
    scale = 1.0 / jnp.sqrt(jnp.float32(head_size))
    offset = jnp.log(jnp.float32(cached * lax.axis_size("seq")))

    def block_sum(query_part, index, mask_part):
        start = index * block
        key_block = lax.dynamic_slice_in_dim(key_local, start, block, 0)
        value_block = lax.dynamic_slice_in_dim(value_local, start, block, 0)
        live = jnp.repeat(jnp.repeat(mask_part, BLK, axis=0), BLK, axis=1) > 0
        score = (
            jnp.einsum("qgd,kd->gqk", query_part, key_block, preferred_element_type=jnp.float32)
            * scale
            - offset
        )
        weight = jnp.where(live[None], jax.nn.sigmoid(score), 0.0).astype(jnp.bfloat16)
        return jnp.einsum("gqk,kd->qgd", weight, value_block, preferred_element_type=jnp.float32)

    def step(index, total):
        mask_part = lax.dynamic_slice_in_dim(mask, index * mask_cols, mask_cols, 1)
        return total + block_sum(query_heads, index, mask_part)

    attended = lax.fori_loop(0, count, step, jnp.zeros((rows, group, head_size), jnp.float32))
    partial_value = attended.reshape(rows, group * head_size)
    own_rows = rows // lax.axis_size("seq")
    summed = lax.psum(partial_value, "seq")
    mine = lax.dynamic_slice_in_dim(summed, lax.axis_index("seq") * own_rows, own_rows, 0)
    attended_bf = mine.astype(jnp.bfloat16)
    terms = jnp.dot(
        attended_bf,
        lax.all_gather(out_proj, "seq", axis=1, tiled=True),
        preferred_element_type=jnp.float32,
    )
    return lax.psum_scatter(terms, "head", scatter_dimension=1, tiled=True).astype(jnp.bfloat16)


def solution(mesh):
    placed = (
        P("seq", "head"),
        P("head", "seq", None),
        P("head", "seq", None),
        P(None, "seq"),
        P("head", "seq"),
    )
    return jax.shard_map(
        on_device, mesh=mesh, in_specs=placed, out_specs=P("seq", "head"), check_vma=False
    )
```

profile of v0, /device:TPU:1, one launch (start us, length us, event | category | flops | bytes accessed | tf_op | source)
XLA Modules:
  0.0 537.1 jit_solution(15371083338233864619)
XLA Ops:
  6.5 0.0 all-gather.3.cloned.1.call-start
  6.5 0.7 all-gather.3.cloned.1.call-update
  7.3 0.0 all-gather.5.cloned.1.call-start
  7.3 0.7 all-gather.5.cloned.1.call-update
  8.0 0.0 reduce-scatter.2.cloned.1.call-start
  8.1 1.2 copy.6
  9.3 135.8 %all-gather.3.cloned.1.call-done = bf16[1024,512]{1,0:T(8,128)(2,1)} async-done(((bf16[16,512]{1,0:T(8,128)(2,1)}), bf16[1024,512]{1,0:T(8,128)(2,1)}) %all-gather.3.cloned.1.call-update) | async-done | bytes 1048592 | tf_op jit(solution)/shard_map/all_gather | solution.py:10
  145.1 2.1 reshape.31
  147.3 37.7 %while.16 = (s32[]{:T(128)}, f32[1024,4,128]{0,2,1:T(8,128)S(1)}, bf16[2048,128]{0,1:T(8,128)(2,1)S(1)}, s32[8,16]{1,0:T(8,128)}, bf16[2048,128]{1,0:T(8,128)(2,...) while((s32[]{:T(128)}, f32[1024,4,128]{0,2,1:T(8,128)S(1)}, ...), condition=%wide.region_1.2_spmd.clone, body=%wide.region_0.1_spmd.clone.sunk | while | flops 1089470464 | bytes 7612318 | solution.py:41
  147.3 0.8 dynamic-slice_compare_fusion.2
  148.1 3.2 broadcast_in_dim.79
  151.2 0.3 copy.17
  151.5 5.1 bitcast_add_fusion.2
  156.7 0.8 dynamic-slice_compare_fusion.2
  157.5 3.2 broadcast_in_dim.79
  160.7 0.3 copy.17
  161.0 5.1 bitcast_add_fusion.2
  166.1 0.8 dynamic-slice_compare_fusion.2
  166.9 3.2 broadcast_in_dim.79
  170.1 0.3 copy.17
  170.4 5.1 bitcast_add_fusion.2
  175.6 0.8 dynamic-slice_compare_fusion.2
  176.4 3.2 broadcast_in_dim.79
  179.5 0.3 copy.17
  179.8 5.1 bitcast_add_fusion.2
  185.0 251.1 %all-reduce.1 = bf16[1024,512]{0,1:T(8,128)(2,1)S(1)} all-reduce(f32[1024,512]{0,1:T(8,128)S(1)} %bitcast.42), channel_id=1, replica_groups=mesh['seq'=64,'head'=8] {'seq'}, use_global_device_ids=true, to_apply=%region_2.3 | all-reduce | flops 524288 | bytes 3145728 | tf_op jit(solution)/shard_map/psum | solution.py:44
  436.1 0.0 all-gather.5.cloned.1.call-done
  436.1 4.2 fusion.21
  440.3 0.0 reduce-scatter.2.cloned.1.call-update
  440.4 88.8 %reduce-scatter.2.cloned.1.call-done = f32[16,512]{1,0:T(8,128)} async-done(((f32[16,4096]{1,0:T(8,128)}), f32[16,512]{1,0:T(8,128)}) %reduce-scatter.2.cloned.1.call-update) | async-done | bytes 32784 | tf_op jit(solution)/shard_map/reduce_scatter | solution.py:52
  529.2 1.4 convert_element_type.17
  (5 shorter events, 0.2 us)
Async XLA Ops:
  6.5 138.6 %all-gather.3.cloned.1.call-start = ((), (), s32[]{:S(2)}) async-start(), calls=%async_computation.1 | async-start | bytes 1064960 | tf_op jit(solution)/shard_map/all_gather | solution.py:10
  7.3 428.9 %all-gather.5.cloned.1.call-start = ((), (), s32[]{:S(2)}) async-start(), calls=%async_computation.2 | async-start | bytes 4259840 | tf_op jit(solution)/shard_map/all_gather | solution.py:49
  8.0 521.2 %reduce-scatter.2.cloned.1.call-start = ((), (), s32[]{:S(2)}) async-start(), calls=%async_computation.3 | async-start | bytes 294912 | tf_op jit(solution)/shard_map/reduce_scatter | solution.py:52
Sparse Core Ops, SparseCore 0:
  10.3 134.7 all-gather.2
  148.1 145.2 all-gather.4
  440.5 88.6 reduce-scatter.1
where the time goes:
time: 538 us; the launch traced here: 537 us
  blocking collectives  251 us (47%)
  waiting for transfers between devices  226 us (42%)
  matrix products  24.8 us (5%)
  local copies, waits for them, and re-layouts  17.3 us (3%)
  between operations  13.2 us (2%)
    psum x1, blocking collectives, on_device(): summed = lax.psum(partial_value, 'seq')  251 us
    all_gather x1, waiting for transfers between devices, on_device(): gathered = lax.all_gather(queries, 'seq', axis=0, tiled=True)  136 us
    reduce_scatter x1, waiting for transfers between devices, on_device(): lax.psum_scatter(terms, 'head', scatter_dimension=1, tiled=True)  88.8 us
    dot_general x4, matrix products, block_sum(): jnp.einsum('gqk,kd->qgd', weight, value_block, preferred_element_type=jnp...  20.6 us
    broadcast_in_dim x8, local copies, waits for them, and re-layouts, block_sum(): live = jnp.repeat(jnp.repeat(mask_part, BLK, axis=0), BLK, axis=1) > 0  12.9 us
  transfers between devices with their start and end apart: 3, of which 2 were waited for; matrix products, arithmetic and copies ran while one was open for 8% of the time, Pallas kernels for 0%

commit v1 on v0

v1 whole, which is shorter than its diff:
```python
import functools
import math

import jax
import jax.numpy as jnp
from jax import lax
from jax.experimental import pallas as pl
from jax.experimental.pallas import tpu as pltpu
from jax.sharding import PartitionSpec as P

MESH = pl.DeviceIdType.MESH
BF = jnp.bfloat16
F32 = jnp.float32

NY, NZ = 4, 16
NH = 8
HD = 128
GROUP = 4
ROWS = 16
KEYS = 2048
BLK = 128
TILE = 256
UNITS = NZ // 2
SCALE = -math.log2(math.e) / math.sqrt(HD)
SHIFT = 2.0**-17


def kernel(
    q_hbm, k_hbm, v_hbm, mask_ref, w_hbm, o_ref,
    k_raw, k2t, v_buf, cm, q_buf, q2, p_send, y_recv, z_send, z_recv,
    a_send, a_recv, w_raw, w_buf, o_send, o_recv,
    loc, qr_s, qr_r, ql_s, ql_r, qy_s, qy_r, ps_s, ps_r, z_s, z_r,
    a_s, a_r, wr_s, wr_r, wl_s, wl_r, o_s, o_r,
):
    seq = lax.axis_index("seq")
    head = lax.axis_index("head")
    y, z = seq // NZ, lax.rem(seq, NZ)

    def zmod(value):
        return lax.rem(value + 2 * NZ, NZ)

    def ypeer(d):
        return lax.rem(y + d, NY)

    def at(yy, zz):
        return yy * NZ + zz

    def remote(src, dst, send, recv, to_seq, to_head):
        return pltpu.make_async_remote_copy(
            src_ref=src, dst_ref=dst, send_sem=send, recv_sem=recv,
            device_id=(to_seq, to_head), device_id_type=MESH,
        )

    right, left = at(y, zmod(z + 1)), at(y, zmod(z - 1))
    out_y = head // 2
    own_out = out_y == y

    q_load = pltpu.make_async_copy(q_hbm, q_buf.at[z, y], loc.at[0])
    k_load = pltpu.make_async_copy(k_hbm.at[0], k_raw, loc.at[1])
    v_load = pltpu.make_async_copy(v_hbm.at[0], v_buf, loc.at[2])
    w_load = pltpu.make_async_copy(w_hbm, w_raw, loc.at[3])
    q_load.start()
    k_load.start()
    w_load.start()
    v_load.start()

    barrier = pltpu.get_barrier_semaphore()

    def greet(to_seq, to_head):
        pl.semaphore_signal(barrier, inc=1, device_id=(to_seq, to_head), device_id_type=MESH)

    for d in range(1, NY):
        greet(at(ypeer(d), z), head)

    def greet_z(d, carry):
        greet(at(y, zmod(z + d)), head)
        return carry

    lax.fori_loop(1, NZ, greet_z, 0)
    for h in range(NH):
        @pl.when(jnp.logical_not(jnp.logical_and(own_out, head == h)))
        def _():
            greet(at(out_y, z), h)

    live = mask_ref[...] > 0
    cut = jnp.where(live, F32(SHIFT), F32(jnp.inf))
    for b in range(KEYS // BLK):
        wide = jnp.broadcast_to(cut[:, b : b + 1], (8, BLK))
        for r in range(8):
            cm[r, :, b * BLK : (b + 1) * BLK] = jnp.broadcast_to(wide[r : r + 1], (8, BLK))
    q_load.wait()
    pl.semaphore_wait(barrier, NY - 1 + NZ - 1 + NH - own_out.astype(jnp.int32))

    def q_ring_r(i, step):
        ref = q_buf.at[zmod(z - i), y]
        return remote(ref, ref, qr_s.at[i], qr_r.at[step], right, head)

    def q_ring_l(i, step):
        ref = q_buf.at[zmod(z + i), y]
        return remote(ref, ref, ql_s.at[i], ql_r.at[step], left, head)

    def q_hand(b):
        ref = q_buf.at[b, y]
        for d in range(1, NY):
            remote(ref, ref, qy_s.at[b], qy_r.at[b], at(ypeer(d), z), head).start()

    def three(b, send, recv):
        ref = y_recv.at[b]
        return remote(ref, ref, send, recv, right, head)

    q_ring_r(0, 0 + 1).start()
    q_ring_l(0, 0 + 1).start()
    q_hand(z)

    k_load.wait()
    keys_t = k_raw[...].T
    k2t[:HD, :] = keys_t
    k2t[HD:, :] = keys_t
    w_load.wait()
    half = w_raw.shape[0] // 2
    w_buf[z] = jnp.concatenate([w_raw[:half, :], w_raw[half:, :]], axis=1)
    v_load.wait()

    def w_ring_r(i, step):
        ref = w_buf.at[zmod(z - i)]
        return remote(ref, ref, wr_s.at[i], wr_r.at[step], right, head)

    def w_ring_l(i, step):
        ref = w_buf.at[zmod(z + i)]
        return remote(ref, ref, wl_s.at[i], wl_r.at[step], left, head)

    w_ring_r(0, 0 + 1).start()
    w_ring_l(0, 0 + 1).start()

    def attend(blocks):
        for n, b in enumerate(blocks):
            for yy in range(NY):
                for g in range(GROUP):
                    part = q_buf[b, yy, :, g * HD : (g + 1) * HD].astype(F32) * SCALE
                    high = part.astype(BF)
                    row = ((n * NY + yy) * GROUP + g) * ROWS
                    q2[row : row + ROWS, :HD] = high
                    q2[row : row + ROWS, HD:] = (part - high.astype(F32)).astype(BF)
        total = jnp.zeros((q2.shape[0], HD), F32)
        span = GROUP * ROWS
        for t in range(KEYS // TILE):
            cols = slice(t * TILE, (t + 1) * TILE)
            score = jnp.dot(q2[...], k2t[:, cols], preferred_element_type=F32)
            power = jnp.exp2(score)
            parts = []
            for n, b in enumerate(blocks):
                for yy in range(NY):
                    row = (n * NY + yy) * span
                    add = cm[yy * 2 + b // 8, :, cols]
                    group = power[row : row + span].reshape(span // 8, 8, TILE) + add[None]
                    parts.append(
                        pltpu.reciprocal(group, approx=True).reshape(span, TILE).astype(BF)
                    )
            weight = jnp.concatenate(parts, axis=0)
            total = total + jnp.dot(weight, v_buf[cols, :], preferred_element_type=F32)
        for n, b in enumerate(blocks):
            for yy in range(NY):
                for g in range(GROUP):
                    row = ((n * NY + yy) * GROUP + g) * ROWS
                    p_send[b, yy, :, g * HD : (g + 1) * HD] = (total[row : row + ROWS] * SHIFT).astype(BF)

    def hand_out(b):
        for d in range(1, NY):
            to = ypeer(d)
            remote(p_send.at[b, to], y_recv.at[b, d - 1], ps_s.at[b], ps_r.at[b], at(to, z), head).start()

    def z_copy(b):
        rel = zmod(b - z)
        return remote(z_send.at[b], z_recv.at[rel - 1], z_s.at[b], z_r, at(y, b), head)

    def gather_up(b, own):
        three(b, ps_s.at[b], ps_r.at[b]).wait_recv()
        total = p_send[b, y].astype(F32)
        for d in range(NY - 1):
            total = total + y_recv[b, d].astype(F32)
        z_send[b] = total.astype(BF)

        @pl.when(jnp.logical_not(own))
        def _():
            z_copy(b).start()

    def unit(u, carry):
        i = u + 1
        q_ring_r_in = zmod(z - i)
        q_ring_r(i, i).wait_recv()

        @pl.when(i < UNITS)
        def _():
            q_ring_r(i, i + 1).start()

        q_hand(q_ring_r_in)

        @pl.when(i < UNITS)
        def _():
            q_ring_l(i, i).wait_recv()

            @pl.when(i < UNITS - 1)
            def _():
                q_ring_l(i, i + 1).start()

            q_hand(zmod(z + i))

        @pl.when(u > 0)
        def _():
            w_ring_r(u, u).wait_recv()
            w_ring_r(u, u + 1).start()
            w_ring_l(u, u).wait_recv()

            @pl.when(u < UNITS - 1)
            def _():
                w_ring_l(u, u + 1).start()

        b0, b1 = zmod(z - i), zmod(z + u)
        three(b0, qy_s.at[b0], qy_r.at[b0]).wait_recv()
        three(b1, qy_s.at[b1], qy_r.at[b1]).wait_recv()
        attend((b0, b1))
        hand_out(b0)
        hand_out(b1)

        @pl.when(u > 0)
        def _():
            gather_up(zmod(z - u), False)
            gather_up(zmod(z + u - 1), u == 1)

        return carry

    lax.fori_loop(0, UNITS, unit, 0)
    gather_up(zmod(z - UNITS), False)
    gather_up(zmod(z + UNITS - 1), False)

    w_ring_r(UNITS, UNITS).wait_recv()

    remote(z_recv, z_recv, z_s.at[0], z_r, right, head).wait_recv()
    total = z_send[z].astype(F32)
    for n in range(NZ - 1):
        total = total + z_recv[n].astype(F32)
    a_send[...] = total.astype(BF)
    for d in range(1, NY):
        remote(a_send, a_recv.at[d - 1], a_s.at[d], a_r, at(ypeer(d), z), head).start()

    def left_all(b, carry):
        three(b, qy_s.at[b], qy_r.at[b]).wait_send()
        three(b, ps_s.at[b], ps_r.at[b]).wait_send()

        @pl.when(b != z)
        def _():
            z_copy(b).wait_send()

        return carry

    lax.fori_loop(0, NZ, left_all, 0)

    def left_ring(i, carry):
        q_ring_r(i, i).wait_send()
        w_ring_r(i, i).wait_send()

        @pl.when(i < UNITS - 1)
        def _():
            q_ring_l(i, i).wait_send()
            w_ring_l(i, i).wait_send()

        return carry

    lax.fori_loop(0, UNITS, left_ring, 0)

    remote(a_recv, a_recv, a_s.at[0], a_r, right, head).wait_recv()

    rows = [a_send[...]] + [a_recv[d] for d in range(NY - 1)]
    attended = jnp.concatenate(rows, axis=0)
    depth = attended.shape[1] // 2
    stacked = jnp.concatenate([attended[:, :depth], attended[:, depth:]], axis=0)
    count = NY * ROWS
    for c in range(2):
        for n in range(0, NZ // 2, 2):
            pair = []
            for m in range(2):
                full = jnp.dot(stacked, w_buf[c * (NZ // 2) + n + m], preferred_element_type=F32)
                pair.append(full[:count, :64] + full[count:, 64:])
            both = jnp.concatenate(pair, axis=1).astype(BF)
            for d in range(NY):
                o_send[d, c, :, n * 64 : (n + 2) * 64] = both[d * ROWS : (d + 1) * ROWS]

    def o_copy(d, c):
        to = lax.rem(y - d + NY, NY)
        return remote(o_send.at[d, c], o_recv.at[head], o_s.at[d, c], o_r, at(to, z), 2 * y + c)

    for d in range(NY):
        for c in range(2):
            if d == 0:
                mine = head == 2 * y + c

                @pl.when(mine)
                def _():
                    pltpu.make_async_copy(o_send.at[d, c], o_recv.at[head], o_r).start()

                @pl.when(jnp.logical_not(mine))
                def _():
                    o_copy(d, c).start()
            else:
                o_copy(d, c).start()

    for d in range(1, NY):
        remote(a_send, a_recv.at[d - 1], a_s.at[d], a_r, right, head).wait_send()
    remote(o_recv, o_recv, o_s.at[0, 0], o_r, right, head).wait_recv()
    total = o_recv[0].astype(F32)
    for n in range(1, NH):
        total = total + o_recv[n].astype(F32)
    o_ref[...] = total.astype(BF)
    for d in range(NY):
        for c in range(2):
            if d == 0:
                @pl.when(head != 2 * y + c)
                def _():
                    o_copy(d, c).wait_send()
            else:
                o_copy(d, c).wait_send()


def on_device(queries, keys, values, mask, out_proj):
    width = queries.shape[1]
    block = (ROWS, width)
    dma = pltpu.SemaphoreType.DMA
    return pl.pallas_call(
        kernel,
        out_shape=jax.ShapeDtypeStruct(block, BF),
        in_specs=[
            pl.BlockSpec(memory_space=pl.ANY),
            pl.BlockSpec(memory_space=pl.ANY),
            pl.BlockSpec(memory_space=pl.ANY),
            pl.BlockSpec(memory_space=pltpu.VMEM),
            pl.BlockSpec(memory_space=pl.ANY),
        ],
        out_specs=pl.BlockSpec(memory_space=pltpu.VMEM),
        scratch_shapes=[
            pltpu.VMEM((KEYS, HD), BF),
            pltpu.VMEM((2 * HD, KEYS), BF),
            pltpu.VMEM((KEYS, HD), BF),
            pltpu.VMEM((8, 8, KEYS), F32),
            pltpu.VMEM((NZ, NY) + block, BF),
            pltpu.VMEM((2 * NY * GROUP * ROWS, 2 * HD), BF),
            pltpu.VMEM((NZ, NY) + block, BF),
            pltpu.VMEM((NZ, NY - 1) + block, BF),
            pltpu.VMEM((NZ,) + block, BF),
            pltpu.VMEM((NZ - 1,) + block, BF),
            pltpu.VMEM(block, BF),
            pltpu.VMEM((NY - 1,) + block, BF),
            pltpu.VMEM(out_proj.shape, BF),
            pltpu.VMEM((NZ, out_proj.shape[0] // 2, 2 * out_proj.shape[1]), BF),
            pltpu.VMEM((NY, 2) + block, BF),
            pltpu.VMEM((NH,) + block, BF),
            dma((4,)),
            dma((UNITS + 1,)), dma((UNITS + 1,)), dma((UNITS + 1,)), dma((UNITS + 1,)),
            dma((NZ,)), dma((NZ,)),
            dma((NZ,)), dma((NZ,)),
            dma((NZ,)), dma,
            dma((NY,)), dma,
            dma((UNITS + 1,)), dma((UNITS + 1,)), dma((UNITS + 1,)), dma((UNITS + 1,)),
            dma((NY, 2)), dma,
        ],
        compiler_params=pltpu.CompilerParams(
            collective_id=0, has_side_effects=True, vmem_limit_bytes=40 * 1024 * 1024
        ),
        name="attend",
    )(queries, keys, values, mask, out_proj)


def solution(mesh):
    placed = (
        P("seq", "head"),
        P("head", "seq", None),
        P("head", "seq", None),
        P(None, "seq"),
        P("head", "seq"),
    )
    return jax.shard_map(
        on_device, mesh=mesh, in_specs=placed, out_specs=P("seq", "head"), check_vma=False
    )
```

time: 538 us -> 95.1 us (0.18)
  blocking collectives: 251 us -> 0 us
  waiting for transfers between devices: 226 us -> 0 us
  Pallas kernels: 0 us -> 89.9 us
  matrix products: 24.8 us -> 0 us
  local copies, waits for them, and re-layouts: 17.3 us -> 3.67 us
  between operations: 13.2 us -> 0.04 us
    psum x1 -> x0, blocking collectives: 251 us -> none  [on_device(): summed = lax.psum(partial_value, 'seq')]
    all_gather x2 -> x0, waiting for transfers between devices: 136 us -> none  [the longest x1 136 us: on_device(): gathered = lax.all_gather(queries, 'seq', axis=0, tiled=True)]
    pallas_call x0 -> x1, Pallas kernels: none -> 89.9 us  [on_device(): pl.pallas_call(kernel, out_shape=jax.ShapeDtypeStruct(block, BF), in_spec...]
    reduce_scatter x1 -> x0, waiting for transfers between devices: 88.8 us -> none  [on_device(): lax.psum_scatter(terms, 'head', scatter_dimension=1, tiled=True)]
    dot_general x5 -> x0, matrix products: 24.8 us -> none  [the longest x4 20.6 us: block_sum(): jnp.einsum('gqk,kd->qgd', weight, value_block, preferred_element_type=jnp...]
    broadcast_in_dim x8 -> x0, local copies, waits for them, and re-layouts: 12.9 us -> none  [block_sum(): live = jnp.repeat(jnp.repeat(mask_part, BLK, axis=0), BLK, axis=1) > 0]
  transfers between devices with their start and end apart: 3 -> 0, of which waited for: 2 -> 0; matrix products, arithmetic and copies ran while one was open for 8% -> 0% of each run, Pallas kernels for 0% -> 0%
where the time goes in v1:
time: 95.1 us; the launch traced here: 93.6 us
  Pallas kernels  89.9 us (95%)
  local copies, waits for them, and re-layouts  3.67 us (4%)
    pallas_call x1, Pallas kernels, on_device(): pl.pallas_call(kernel, out_shape=jax.ShapeDtypeStruct(block, BF), in_spec...  89.9 us
    unnamed x10, local copies, waits for them, and re-layouts  3.67 us

profile of v1, /device:TPU:1, one launch (start us, length us, event | category | flops | bytes accessed | tf_op | source)
XLA Modules:
  0.0 93.6 jit_solution(10906157563493218455)
XLA Ops:
  0.0 0.0 copy-start.3
  0.0 0.0 copy-start.2
  0.0 1.0 %copy.6.w_hbm = bf16[512,64]{1,0:T(8,128)(2,1)S(1)} copy(bf16[512,64]{0,1:T(8,128)(2,1)} %param.9) | data formatting | bytes 131072 | tf_op args[4]
  1.0 0.0 copy-done.3
  1.0 0.0 copy-done.2
  1.0 0.0 copy-start
  1.0 1.0 %copy-done = bf16[1,2048,128]{2,1,0:T(8,128)(2,1)S(1)} copy-done((bf16[1,2048,128]{2,1,0:T(8,128)(2,1)S(1)}, bf16[1,2048,128]{2,1,0:T(8,128)(2,1)}, u32[]{:S(2)}) %copy-start) | copy-done | bytes 524312
  2.1 0.0 copy-start.1
  2.1 1.0 %copy-done.1 = bf16[1,2048,128]{2,1,0:T(8,128)(2,1)S(1)} copy-done((bf16[1,2048,128]{2,1,0:T(8,128)(2,1)S(1)}, bf16[1,2048,128]{2,1,0:T(8,128)(2,1)}, u32[]{:S(2)}) %copy-start.1) | copy-done | bytes 524312
  3.1 89.9 %attend.1 = bf16[16,512]{1,0:T(8,128)(2,1)S(1)} custom-call(bf16[16,512]{1,0:T(8,128)(2,1)S(1)} %copy-done.2, bf16[1,2048,128]{2,1,0:T(8,128)(2,1)S(1)} %copy-done, bf16[1,2048,128]{2,1,0:T(8,128)(2,1)S(1)} %copy-done.1, s32[8,16]{1,0:T(8,128)S(1)} %copy-done.3, bf16[512,64]{1,0:T(8,128)(2,1)S(1)} %copy.6.w_hbm), custom_call_target="tpu_custom_call" | custom-call | tf_op jit(solution)/shard_map/attend/pallas_call | solution.py:328
  93.0 0.6 copy.8
Async XLA Ops:
  0.0 1.0 %copy-start.3 = (s32[8,16]{1,0:T(8,128)S(1)}, s32[8,16]{1,0:T(8,128)}, u32[]{:S(2)}) copy-start(s32[8,16]{1,0:T(8,128)} %mask_ref.1) | copy-start | bytes 1540
  0.0 1.0 %copy-start.2 = (bf16[16,512]{1,0:T(8,128)(2,1)S(1)}, bf16[16,512]{1,0:T(8,128)(2,1)}, u32[]{:S(2)}) copy-start(bf16[16,512]{1,0:T(8,128)(2,1)} %q_hbm.1) | copy-start | bytes 49156
  1.0 1.0 %copy-start = (bf16[1,2048,128]{2,1,0:T(8,128)(2,1)S(1)}, bf16[1,2048,128]{2,1,0:T(8,128)(2,1)}, u32[]{:S(2)}) copy-start(bf16[1,2048,128]{2,1,0:T(8,128)(2,1)} %k_hbm.1) | copy-start | bytes 1572868
  2.1 1.0 %copy-start.1 = (bf16[1,2048,128]{2,1,0:T(8,128)(2,1)S(1)}, bf16[1,2048,128]{2,1,0:T(8,128)(2,1)}, u32[]{:S(2)}) copy-start(bf16[1,2048,128]{2,1,0:T(8,128)(2,1)} %v_hbm.1) | copy-start | bytes 1572868

commit v2 on v1

v2 whole, which is shorter than its diff:
```python
import functools
import math

import jax
import jax.numpy as jnp
from jax import lax
from jax.experimental import pallas as pl
from jax.experimental.pallas import tpu as pltpu
from jax.sharding import PartitionSpec as P

MESH = pl.DeviceIdType.MESH
BF = jnp.bfloat16
F32 = jnp.float32

NY, NZ = 4, 16
NH = 8
HD = 128
GROUP = 4
ROWS = 16
KEYS = 2048
BLK = 128
TILE = 256
UNITS = NZ // 2
SCALE = -math.log2(math.e) / math.sqrt(HD)
SHIFT = 2.0**-17


FIRST = (0, 3, 8, -6, 4, 5, 7, -1)
SECOND = (1, -3, 6, 2, -4, -5, -7, -2)
LAG = 3


def kernel(
    q_hbm, k_hbm, v_hbm, mask_ref, w_hbm, o_ref,
    k2, v_buf, cm, q_buf, q2, p_send, y_recv, z_send, z_recv,
    a_send, a_recv, w_buf, o_send, o_recv,
    loc, qz_s, qz_r, qf_s, qy_s, qy_r, ps_s, ps_r, z_s, z_r,
    a_s, a_r, w_s, wr_r, wl_r, o_s, o_r,
):
    seq = lax.axis_index("seq")
    head = lax.axis_index("head")
    y, z = seq // NZ, lax.rem(seq, NZ)

    def zmod(value):
        return lax.rem(value + 2 * NZ, NZ)

    def ypeer(d):
        return lax.rem(y + d, NY)

    def at(yy, zz):
        return yy * NZ + zz

    def remote(src, dst, send, recv, to_seq, to_head):
        return pltpu.make_async_remote_copy(
            src_ref=src, dst_ref=dst, send_sem=send, recv_sem=recv,
            device_id=(to_seq, to_head), device_id_type=MESH,
        )

    right, left = at(y, zmod(z + 1)), at(y, zmod(z - 1))
    out_y = head // 2
    own_out = out_y == y

    def arrived(ref, sem):
        remote(ref, ref, o_s, sem, right, head).wait_recv()

    def left_here(ref, sem):
        remote(ref, ref, sem, o_r, right, head).wait_send()

    k_load = pltpu.make_async_copy(k_hbm.at[0], k2.at[:, :HD], loc.at[1])
    k_again = pltpu.make_async_copy(k_hbm.at[0], k2.at[:, HD:], loc.at[2])
    q_load = pltpu.make_async_copy(q_hbm, q_buf.at[z, y], loc.at[0])
    v_load = pltpu.make_async_copy(v_hbm.at[0], v_buf, loc.at[3])
    w_load = pltpu.make_async_copy(w_hbm, w_buf.at[z], loc.at[4])
    q_load.start()
    w_load.start()
    k_load.start()
    k_again.start()
    v_load.start()

    barrier = pltpu.get_barrier_semaphore()

    def greet(to_seq, to_head):
        pl.semaphore_signal(barrier, inc=1, device_id=(to_seq, to_head), device_id_type=MESH)

    for d in range(1, NY):
        greet(at(ypeer(d), z), head)

    def greet_z(d, carry):
        greet(at(y, zmod(z + d)), head)
        return carry

    lax.fori_loop(1, NZ, greet_z, 0)
    for h in range(NH):
        @pl.when(jnp.logical_not(jnp.logical_and(own_out, head == h)))
        def _():
            greet(at(out_y, z), h)

    live = mask_ref[...] > 0
    cut = jnp.where(live, F32(SHIFT), F32(jnp.inf))
    for b in range(KEYS // BLK):
        wide = jnp.broadcast_to(cut[:, b : b + 1], (8, BLK))
        for r in range(8):
            cm[r, :, b * BLK : (b + 1) * BLK] = jnp.broadcast_to(wide[r : r + 1], (8, BLK))
    q_load.wait()
    pl.semaphore_wait(barrier, NY - 1 + NZ - 1 + NH - own_out.astype(jnp.int32))

    def q_copy(b, send, d):
        ref = q_buf.at[b, y]
        return remote(ref, ref, send, qz_r.at[b], at(y, zmod(z + d)), head)

    def q_hand(b):
        ref = q_buf.at[b, y]
        for d in range(1, NY):
            remote(ref, ref, qy_s, qy_r.at[b], at(ypeer(d), z), head).start()

    def q_take(offset, relay):
        b = zmod(z + offset)
        arrived(q_buf.at[b, y], qz_r.at[b])
        if relay:
            q_copy(b, qf_s, 1).start()
            q_copy(b, qf_s, -1).start()
        q_hand(b)

    for d in (1, -1, 3, -3):
        q_copy(z, qz_s, d).start()
    q_hand(z)
    for d in (6, -6, 8):
        q_copy(z, qz_s, d).start()

    def w_ring_r(i):
        ref = w_buf.at[zmod(z - i)]
        remote(ref, ref, w_s, wr_r.at[i + 1], right, head).start()

    def w_ring_l(i):
        ref = w_buf.at[zmod(z + i)]
        remote(ref, ref, w_s, wl_r.at[i + 1], left, head).start()

    def w_relay(i):
        arrived(w_buf.at[zmod(z - i)], wr_r.at[i])
        if i < UNITS:
            w_ring_r(i)
            arrived(w_buf.at[zmod(z + i)], wl_r.at[i])
        if i < UNITS - 1:
            w_ring_l(i)

    w_load.wait()
    w_ring_r(0)
    w_ring_l(0)

    k_load.wait()
    k_again.wait()
    v_load.wait()
    q_take(1, False)
    q_take(-1, False)
    q_take(3, True)
    q_take(-3, True)
    w_relay(1)

    def attend(blocks):
        for n, b in enumerate(blocks):
            for yy in range(NY):
                for g in range(GROUP):
                    part = q_buf[b, yy, :, g * HD : (g + 1) * HD].astype(F32) * SCALE
                    high = part.astype(BF)
                    row = ((n * NY + yy) * GROUP + g) * ROWS
                    q2[row : row + ROWS, :HD] = high
                    q2[row : row + ROWS, HD:] = (part - high.astype(F32)).astype(BF)
        total = jnp.zeros((q2.shape[0], HD), F32)
        span = GROUP * ROWS
        for t in range(KEYS // TILE):
            cols = slice(t * TILE, (t + 1) * TILE)
            score = lax.dot_general(q2[...], k2[cols, :], (((1,), (1,)), ((), ())), preferred_element_type=F32)
            power = jnp.exp2(score)
            parts = []
            for n, b in enumerate(blocks):
                for yy in range(NY):
                    row = (n * NY + yy) * span
                    add = cm[yy * 2 + b // 8, :, cols]
                    group = power[row : row + span].reshape(span // 8, 8, TILE) + add[None]
                    parts.append(
                        pltpu.reciprocal(group, approx=True).reshape(span, TILE).astype(BF)
                    )
            weight = jnp.concatenate(parts, axis=0)
            total = total + jnp.dot(weight, v_buf[cols, :], preferred_element_type=F32)
        for n, b in enumerate(blocks):
            for yy in range(NY):
                for g in range(GROUP):
                    row = ((n * NY + yy) * GROUP + g) * ROWS
                    p_send[b, yy, :, g * HD : (g + 1) * HD] = (total[row : row + ROWS] * SHIFT).astype(BF)

    def hand_out(b):
        for d in range(1, NY):
            to = ypeer(d)
            remote(p_send.at[b, to], y_recv.at[b, d - 1], ps_s, ps_r.at[b], at(to, z), head).start()

    def gather_up(b, own):
        arrived(y_recv.at[b], ps_r.at[b])
        total = p_send[b, y].astype(F32)
        for d in range(NY - 1):
            total = total + y_recv[b, d].astype(F32)
        z_send[b] = total.astype(BF)

        @pl.when(jnp.logical_not(own))
        def _():
            rel = zmod(b - z)
            remote(z_send.at[b], z_recv.at[rel - 1], z_s, z_r, at(y, b), head).start()

    def pick(u, table):
        value = jnp.int32(table[0])
        for n in range(1, UNITS):
            value = jnp.where(u == n, table[n], value)
        return zmod(z + value)

    def gather_unit(u):
        gather_up(pick(u, FIRST), u == 0)
        gather_up(pick(u, SECOND), False)

    def unit(u, carry):
        b0, b1 = pick(u, FIRST), pick(u, SECOND)
        arrived(y_recv.at[b0], qy_r.at[b0])
        arrived(y_recv.at[b1], qy_r.at[b1])
        attend((b0, b1))
        hand_out(b0)
        hand_out(b1)

        @pl.when(u == 0)
        def _():
            q_take(8, False)
            q_take(6, True)
            q_take(-6, True)
            for d in (2, -2, 4, -4):
                q_take(d, False)

        @pl.when(u == 1)
        def _():
            w_relay(2)

        @pl.when(u == 2)
        def _():
            for d in (5, -5, 7, -7):
                q_take(d, False)

        @pl.when(u == 3)
        def _():
            w_relay(3)

        @pl.when(u == 5)
        def _():
            w_relay(4)

        @pl.when(u >= LAG)
        def _():
            gather_unit(u - LAG)

        return carry

    lax.fori_loop(0, UNITS, unit, 0)
    w_relay(5)

    def collect(u, carry):
        gather_unit(u)
        return carry

    lax.fori_loop(UNITS - LAG, UNITS, collect, 0)
    w_relay(6)

    arrived(z_recv, z_r)
    total = z_send[z].astype(F32)
    for n in range(NZ - 1):
        total = total + z_recv[n].astype(F32)
    a_send[...] = total.astype(BF)
    for d in range(1, NY):
        remote(a_send, a_recv.at[d - 1], a_s, a_r, at(ypeer(d), z), head).start()
    w_relay(7)

    left_here(z_recv.at[: 7], qz_s)
    left_here(z_recv.at[: 8], qf_s)
    left_here(y_recv, qy_s)
    left_here(y_recv, ps_s)
    left_here(z_recv, z_s)
    arrived(a_recv, a_r)
    w_relay(8)

    rows = [a_send[...]] + [a_recv[d] for d in range(NY - 1)]
    attended = jnp.concatenate(rows, axis=0)
    wide = NZ // 2
    for c in range(2):
        columns = w_buf[c * wide : (c + 1) * wide].reshape(wide * w_buf.shape[1], w_buf.shape[2])
        share = lax.dot_general(attended, columns, (((1,), (1,)), ((), ())), preferred_element_type=F32)
        share = share.astype(BF)
        for d in range(NY):
            o_send[d, c] = share[d * ROWS : (d + 1) * ROWS]
            to = lax.rem(y - d + NY, NY)
            copy = remote(o_send.at[d, c], o_recv.at[head], o_s, o_r, at(to, z), 2 * y + c)
            if d == 0:
                mine = head == 2 * y + c

                @pl.when(mine)
                def _():
                    pltpu.make_async_copy(o_send.at[d, c], o_recv.at[head], o_r).start()

                @pl.when(jnp.logical_not(mine))
                def _():
                    copy.start()
            else:
                copy.start()

    left_here(a_recv, a_s)
    left_here(w_buf.at[: NZ - 1], w_s)
    arrived(o_recv, o_r)
    total = o_recv[0].astype(F32)
    for n in range(1, NH):
        total = total + o_recv[n].astype(F32)
    o_ref[...] = total.astype(BF)

    @pl.when(own_out)
    def _():
        left_here(o_recv.at[: NH - 1], o_s)

    @pl.when(jnp.logical_not(own_out))
    def _():
        left_here(o_recv, o_s)


def on_device(queries, keys, values, mask, out_proj):
    width = queries.shape[1]
    block = (ROWS, width)
    dma = pltpu.SemaphoreType.DMA
    return pl.pallas_call(
        kernel,
        out_shape=jax.ShapeDtypeStruct(block, BF),
        in_specs=[
            pl.BlockSpec(memory_space=pl.ANY),
            pl.BlockSpec(memory_space=pl.ANY),
            pl.BlockSpec(memory_space=pl.ANY),
            pl.BlockSpec(memory_space=pltpu.VMEM),
            pl.BlockSpec(memory_space=pl.ANY),
        ],
        out_specs=pl.BlockSpec(memory_space=pltpu.VMEM),
        scratch_shapes=[
            pltpu.VMEM((KEYS, 2 * HD), BF),
            pltpu.VMEM((KEYS, HD), BF),
            pltpu.VMEM((8, 8, KEYS), F32),
            pltpu.VMEM((NZ, NY) + block, BF),
            pltpu.VMEM((2 * NY * GROUP * ROWS, 2 * HD), BF),
            pltpu.VMEM((NZ, NY) + block, BF),
            pltpu.VMEM((NZ, NY - 1) + block, BF),
            pltpu.VMEM((NZ,) + block, BF),
            pltpu.VMEM((NZ - 1,) + block, BF),
            pltpu.VMEM(block, BF),
            pltpu.VMEM((NY - 1,) + block, BF),
            pltpu.VMEM((NZ,) + out_proj.shape[::-1], BF),
            pltpu.VMEM((NY, 2) + block, BF),
            pltpu.VMEM((NH,) + block, BF),
            dma((5,)),
            dma, dma((NZ,)), dma,
            dma, dma((NZ,)),
            dma, dma((NZ,)),
            dma, dma,
            dma, dma,
            dma, dma((UNITS + 1,)), dma((UNITS + 1,)),
            dma, dma,
        ],
        compiler_params=pltpu.CompilerParams(
            collective_id=0, has_side_effects=True, vmem_limit_bytes=60 * 1024 * 1024
        ),
        name="attend",
    )(queries, keys, values, mask, out_proj.T)


def solution(mesh):
    placed = (
        P("seq", "head"),
        P("head", "seq", None),
        P("head", "seq", None),
        P(None, "seq"),
        P("head", "seq"),
    )
    return jax.shard_map(
        on_device, mesh=mesh, in_specs=placed, out_specs=P("seq", "head"), check_vma=False
    )
```

time: 95.1 us -> 71.7 us (0.75); the launches traced: 93.6 us -> 71.4 us
  Pallas kernels: 89.9 us -> 70.1 us
  local copies, waits for them, and re-layouts: 3.67 us -> 1.32 us
    pallas_call x1, Pallas kernels: 89.9 us -> 70.1 us  [on_device(): pl.pallas_call(kernel, out_shape=jax.ShapeDtypeStruct(block, BF), in_spec...]
    unnamed x10 -> x1, local copies, waits for them, and re-layouts: 3.67 us -> 1.32 us
where the time goes in v2:
time: 71.7 us; the launch traced here: 71.4 us
  Pallas kernels  70.1 us (98%)
  local copies, waits for them, and re-layouts  1.32 us (2%)
    pallas_call x1, Pallas kernels, on_device(): pl.pallas_call(kernel, out_shape=jax.ShapeDtypeStruct(block, BF), in_spec...  70.1 us

profile of v2, /device:TPU:1, one launch (start us, length us, event | category | flops | bytes accessed | tf_op | source)
XLA Modules:
  0.0 71.4 jit_solution(3543674646817438153)
XLA Ops:
  0.0 70.1 %attend.1 = bf16[16,512]{1,0:T(8,128)(2,1)} custom-call(bf16[16,512]{1,0:T(8,128)(2,1)} %q_hbm.1, bf16[1,2048,128]{2,1,0:T(8,128)(2,1)} %k_hbm.1, bf16[1,2048,128]{2,1,0:T(8,128)(2,1)} %v_hbm.1, s32[8,16]{1,0:T(8,128)} %mask_ref.1, bf16[64,512]{1,0:T(8,128)(2,1)} %bitcast.1), custom_call_target="tpu_custom_call" | custom-call | tf_op jit(solution)/shard_map/attend/pallas_call | solution.py:329
  70.1 1.3 %copy.7 = bf16[16,512]{1,0:T(8,128)(2,1)} copy(bf16[16,512]{1,0:T(8,128)(2,1)} %attend.1) | data formatting | bytes 32768

commit v3 on v2

v3 whole, which is shorter than its diff:
```python
import functools
import math

import jax
import jax.numpy as jnp
from jax import lax
from jax.experimental import pallas as pl
from jax.experimental.pallas import tpu as pltpu
from jax.sharding import PartitionSpec as P

MESH = pl.DeviceIdType.MESH
BF = jnp.bfloat16
F32 = jnp.float32

NY, NZ = 4, 16
NX = 4
HD = 128
GROUP = 4
ROWS = 16
KEYS = 2048
BLK = 128
TILE = 256
UNITS = NZ // 2
SCALE = -math.log2(math.e) / math.sqrt(HD)
SHIFT = 2.0**-17


FIRST = (0, 5, 8, 7, 6, 4, 3, -1)
SECOND = (1, -5, -2, -7, -6, -4, -3, 2)
LAST = (FIRST[-1], SECOND[-1])
FAR = (6, 7)
SLOTS = (1, -2, 3, -3, 8, 4, -4, 5, -5)
NEAR = (1, -1, 2, -2, 3, -3, 4, -4, 5, -5, 8)
LAG = 2


def kernel(
    q_hbm, k_hbm, v_hbm, mask_hbm, w_hbm, o_ref,
    m_buf, k2, v_buf, cm, q_buf, q2, p_send, y_recv, z_send, z_recv, n_recv, d_recv,
    a_send, a_recv, w_buf, c_send, c_recv, o_send, o_recv,
    loc, qz_s, qz_r, qf_s, qb_s, qb_r, qy_s, qy_r, ps_s, ps_r, z_s, z_r, n_s, n_r, d_s, d_r,
    a_s, a_r, w_s, wr_r, wl_r, c_s, c_r, o_s, o_r,
):
    seq = lax.axis_index("seq")
    head = lax.axis_index("head")
    y, z = seq // NZ, lax.rem(seq, NZ)

    def zmod(value):
        return lax.rem(value + 2 * NZ, NZ)

    def ypeer(d):
        return lax.rem(y + d, NY)

    def at(yy, zz):
        return yy * NZ + zz

    def remote(src, dst, send, recv, to_seq, to_head):
        return pltpu.make_async_remote_copy(
            src_ref=src, dst_ref=dst, send_sem=send, recv_sem=recv,
            device_id=(to_seq, to_head), device_id_type=MESH,
        )

    right, left = at(y, zmod(z + 1)), at(y, zmod(z - 1))
    x, core = head // 2, lax.rem(head, 2)
    partner = head + 1 - 2 * core
    out_y = x
    own_out = out_y == y

    def arrived(ref, sem):
        remote(ref, ref, o_s, sem, right, head).wait_recv()

    def left_here(ref, sem):
        remote(ref, ref, sem, o_r, right, head).wait_send()

    k_load = pltpu.make_async_copy(k_hbm.at[0], k2.at[:, :HD], loc.at[1])
    k_again = pltpu.make_async_copy(k_hbm.at[0], k2.at[:, HD:], loc.at[2])
    q_load = pltpu.make_async_copy(q_hbm, q_buf.at[z, y], loc.at[0])
    v_load = pltpu.make_async_copy(v_hbm.at[0], v_buf, loc.at[3])
    m_load = pltpu.make_async_copy(mask_hbm, m_buf, loc.at[5])
    w_load = pltpu.make_async_copy(w_hbm, w_buf.at[z], loc.at[4])
    q_load.start()
    m_load.start()
    w_load.start()
    k_load.start()
    k_again.start()
    v_load.start()

    barrier = pltpu.get_barrier_semaphore()

    def greet(to_seq, to_head):
        pl.semaphore_signal(barrier, inc=1, device_id=(to_seq, to_head), device_id_type=MESH)

    for d in range(1, NY):
        greet(at(ypeer(d), z), head)

    for d in NEAR:
        greet(at(y, zmod(z + d)), head)
    for d in range(1, NY):
        for offset in LAST:
            greet(at(ypeer(d), zmod(z - offset)), head)
    greet(seq, partner)
    for n in range(NX):
        @pl.when(jnp.logical_not(jnp.logical_and(own_out, x == n)))
        def _():
            greet(at(out_y, z), 2 * n + core)

    m_load.wait()
    live = m_buf[...] > 0
    cut = jnp.where(live, F32(SHIFT), F32(jnp.inf))
    for b in range(KEYS // BLK):
        wide = jnp.broadcast_to(cut[:, b : b + 1], (8, BLK))
        for r in range(8):
            cm[r, :, b * BLK : (b + 1) * BLK] = jnp.broadcast_to(wide[r : r + 1], (8, BLK))
    q_load.wait()
    pl.semaphore_wait(barrier, NY - 1 + len(NEAR) + len(LAST) * (NY - 1) + 1 + NX - own_out.astype(jnp.int32))

    def q_copy(b, send, d):
        ref = q_buf.at[b, y]
        return remote(ref, ref, send, qz_r.at[b], at(y, zmod(z + d)), head)

    def q_hand(b):
        ref = q_buf.at[b, y]
        for d in range(1, NY):
            remote(ref, ref, qy_s, qy_r.at[b], at(ypeer(d), z), head).start()

    def q_take(offset):
        b = zmod(z + offset)
        arrived(q_buf.at[b, y], qz_r.at[b])
        if offset in (5, -5):
            for d in (2, 1, -1):
                q_copy(b, qf_s, d if offset < 0 else -d).start()
        q_hand(b)

    def q_pass(b, to):
        ref = q_buf.at[b]
        remote(ref, ref, qb_s, qb_r.at[b], to, head).start()

    def q_ring(i):
        for b, to in ((zmod(z - i), right), (zmod(z + i), left)):
            arrived(q_buf.at[b], qb_r.at[b])
            if i < 3:
                q_pass(b, to)

    for d in (5, -5):
        q_copy(z, qz_s, d).start()
    q_hand(z)
    q_copy(z, qz_s, 8).start()

    def w_ring_r(i):
        ref = w_buf.at[zmod(z - i)]
        remote(ref, ref, w_s, wr_r.at[i + 1], right, head).start()

    def w_ring_l(i):
        ref = w_buf.at[zmod(z + i)]
        remote(ref, ref, w_s, wl_r.at[i + 1], left, head).start()

    def w_relay(i):
        arrived(w_buf.at[zmod(z - i)], wr_r.at[i])
        if i < UNITS:
            w_ring_r(i)
            arrived(w_buf.at[zmod(z + i)], wl_r.at[i])
        if i < UNITS - 1:
            w_ring_l(i)

    w_load.wait()
    w_ring_r(0)
    w_ring_l(0)

    k_load.wait()
    k_again.wait()
    v_load.wait()
    arrived(y_recv.at[z], qy_r.at[z])
    q_pass(z, right)
    q_pass(z, left)
    w_relay(1)
    q_take(5)
    q_take(-5)
    q_ring(1)

    def attend(blocks):
        for n, b in enumerate(blocks):
            for yy in range(NY):
                for g in range(GROUP):
                    part = q_buf[b, yy, :, g * HD : (g + 1) * HD].astype(F32) * SCALE
                    high = part.astype(BF)
                    row = ((n * NY + yy) * GROUP + g) * ROWS
                    q2[row : row + ROWS, :HD] = high
                    q2[row : row + ROWS, HD:] = (part - high.astype(F32)).astype(BF)
        total = jnp.zeros((q2.shape[0], HD), F32)
        span = GROUP * ROWS
        for t in range(KEYS // TILE):
            cols = slice(t * TILE, (t + 1) * TILE)
            score = lax.dot_general(q2[...], k2[cols, :], (((1,), (1,)), ((), ())), preferred_element_type=F32)
            power = jnp.exp2(score)
            parts = []
            for n, b in enumerate(blocks):
                for yy in range(NY):
                    row = (n * NY + yy) * span
                    add = cm[yy * 2 + b // 8, :, cols]
                    group = power[row : row + span].reshape(span // 8, 8, TILE) + add[None]
                    parts.append(
                        pltpu.reciprocal(group, approx=True).reshape(span, TILE).astype(BF)
                    )
            weight = jnp.concatenate(parts, axis=0)
            total = total + jnp.dot(weight, v_buf[cols, :], preferred_element_type=F32)
        for n, b in enumerate(blocks):
            for yy in range(NY):
                for g in range(GROUP):
                    row = ((n * NY + yy) * GROUP + g) * ROWS
                    p_send[b, yy, :, g * HD : (g + 1) * HD] = (total[row : row + ROWS] * SHIFT).astype(BF)

    def hand_out(b):
        for d in range(1, NY):
            to = ypeer(d)
            remote(p_send.at[b, to], y_recv.at[b, d - 1], ps_s, ps_r.at[b], at(to, z), head).start()

    def add_up(b, total):
        total = total + p_send[b, y].astype(F32)
        for d in range(NY - 1):
            total = total + y_recv[b, d].astype(F32)
        z_send[b] = total.astype(BF)

    def to_owner(b, offset):
        remote(z_send.at[b], z_recv.at[SLOTS.index(offset)], z_s, z_r, at(y, b), head).start()

    def gather_up(b, u, table):
        arrived(y_recv.at[b], ps_r.at[b])
        add_up(b, jnp.zeros(z_send.shape[1:], F32))
        for n, offset in enumerate(table):
            if offset in (0, 5, -5) or n == UNITS - 1:
                continue

            @pl.when(u == n)
            def _(offset=offset):
                if abs(offset) in FAR:
                    side = int(offset < 0)
                    node = at(y, zmod(b + (5 if side else -5)))
                    slot = n_recv.at[side, FAR.index(abs(offset))]
                    remote(z_send.at[b], slot, n_s, n_r.at[side], node, head).start()
                else:
                    to_owner(b, offset)

    def gather_far(side):
        b = zmod(z + (-5 if side else 5))
        arrived(y_recv.at[b], ps_r.at[b])
        arrived(n_recv.at[side], n_r.at[side])
        total = n_recv[side, 0].astype(F32)
        for n in range(1, len(FAR)):
            total = total + n_recv[side, n].astype(F32)
        add_up(b, total)
        to_owner(b, -5 if side else 5)

    def pick(u, table):
        value = jnp.int32(table[0])
        for n in range(1, UNITS):
            value = jnp.where(u == n, table[n], value)
        return zmod(z + value)

    def gather_unit(u):
        @pl.when(u != 1)
        def _():
            gather_up(pick(u, FIRST), u, FIRST)
            gather_up(pick(u, SECOND), u, SECOND)

    def unit(u, carry):
        b0, b1 = pick(u, FIRST), pick(u, SECOND)

        @pl.when(jnp.logical_and(u >= 1, u <= 5))
        def _():
            arrived(y_recv.at[b0], qy_r.at[b0])

            @pl.when(u != 2)
            def _():
                arrived(y_recv.at[b1], qy_r.at[b1])

        attend((b0, b1))

        @pl.when(u < UNITS - 1)
        def _():
            hand_out(b0)
            hand_out(b1)

        @pl.when(u == UNITS - 1)
        def _():
            for n, b in enumerate((b0, b1)):
                for d in range(NY):
                    to = ypeer(d)
                    remote(p_send.at[b, to], d_recv.at[n, d], d_s, d_r, at(to, b), head).start()

        @pl.when(u == 0)
        def _():
            for d in (8, 7, -7):
                q_take(d)
            w_relay(2)

        @pl.when(u == 1)
        def _():
            for d in (6, -6, 4, -4):
                q_take(d)
            q_ring(2)

        @pl.when(u == 2)
        def _():
            w_relay(3)

        @pl.when(u == 4)
        def _():
            w_relay(4)

        @pl.when(u == 5)
        def _():
            q_ring(3)

        @pl.when(u == 6)
        def _():
            w_relay(5)

        @pl.when(u >= LAG)
        def _():
            gather_unit(u - LAG)

        return carry

    lax.fori_loop(0, UNITS, unit, 0)
    w_relay(6)

    for side in range(2):
        gather_far(side)
    gather_unit(UNITS - 2)
    w_relay(7)

    arrived(z_recv, z_r)
    arrived(d_recv, d_r)
    total = z_send[z].astype(F32)
    for n in range(len(LAST)):
        for d in range(NY):
            total = total + d_recv[n, d].astype(F32)
    for n in range(len(SLOTS)):
        total = total + z_recv[n].astype(F32)
    a_send[...] = total.astype(BF)
    for d in range(1, NY):
        remote(a_send, a_recv.at[d - 1], a_s, a_r, at(ypeer(d), z), head).start()

    left_here(z_recv.at[:3], qz_s)
    left_here(z_recv.at[:6], qf_s)
    left_here(y_recv.at[:8], qb_s)
    left_here(y_recv.at[:10], qy_s)
    left_here(n_recv, n_s)
    left_here(y_recv.at[: NZ - len(LAST)], ps_s)
    left_here(d_recv, d_s)
    left_here(z_recv, z_s)
    arrived(a_recv, a_r)
    w_relay(8)

    rows = [a_send[...]] + [a_recv[d] for d in range(NY - 1)]
    attended = jnp.concatenate(rows, axis=0)
    wide = NZ // 2

    def project(c):
        columns = w_buf[pl.ds(c * wide, wide)].reshape(wide * w_buf.shape[1], w_buf.shape[2])
        return lax.dot_general(attended, columns, (((1,), (1,)), ((), ())), preferred_element_type=F32)

    c_send[...] = project(1 - core).astype(BF)
    swap = remote(c_send, c_recv, c_s, c_r, seq, partner)
    swap.start()
    share = project(core)
    swap.wait_recv()
    o_send[...] = (share + c_recv[...].astype(F32)).astype(BF).reshape(o_send.shape)
    for d in range(NY):
        to = lax.rem(y - d + NY, NY)
        copy = remote(o_send.at[d], o_recv.at[x], o_s, o_r, at(to, z), 2 * y + core)
        if d == 0:
            @pl.when(own_out)
            def _():
                pltpu.make_async_copy(o_send.at[0], o_recv.at[x], o_r).start()

            @pl.when(jnp.logical_not(own_out))
            def _():
                copy.start()
        else:
            copy.start()

    swap.wait_send()
    left_here(a_recv, a_s)
    left_here(w_buf.at[: NZ - 1], w_s)
    arrived(o_recv, o_r)
    total = o_recv[0].astype(F32)
    for n in range(1, NX):
        total = total + o_recv[n].astype(F32)
    o_ref[...] = total.astype(BF)

    @pl.when(own_out)
    def _():
        left_here(o_recv.at[: NX - 1], o_s)

    @pl.when(jnp.logical_not(own_out))
    def _():
        left_here(o_recv, o_s)


def on_device(queries, keys, values, mask, out_proj):
    width = queries.shape[1]
    block = (ROWS, width)
    dma = pltpu.SemaphoreType.DMA
    return pl.pallas_call(
        kernel,
        out_shape=jax.ShapeDtypeStruct(block, BF),
        in_specs=[pl.BlockSpec(memory_space=pltpu.HBM)] * 5,
        out_specs=pl.BlockSpec(memory_space=pltpu.VMEM),
        scratch_shapes=[
            pltpu.VMEM(mask.shape, mask.dtype),
            pltpu.VMEM((KEYS, 2 * HD), BF),
            pltpu.VMEM((KEYS, HD), BF),
            pltpu.VMEM((8, 8, KEYS), F32),
            pltpu.VMEM((NZ, NY) + block, BF),
            pltpu.VMEM((2 * NY * GROUP * ROWS, 2 * HD), BF),
            pltpu.VMEM((NZ, NY) + block, BF),
            pltpu.VMEM((NZ, NY - 1) + block, BF),
            pltpu.VMEM((NZ,) + block, BF),
            pltpu.VMEM((len(SLOTS),) + block, BF),
            pltpu.VMEM((2, len(FAR)) + block, BF),
            pltpu.VMEM((len(LAST), NY) + block, BF),
            pltpu.VMEM(block, BF),
            pltpu.VMEM((NY - 1,) + block, BF),
            pltpu.VMEM((NZ,) + out_proj.shape[::-1], BF),
            pltpu.VMEM((NY * ROWS, width), BF),
            pltpu.VMEM((NY * ROWS, width), BF),
            pltpu.VMEM((NY,) + block, BF),
            pltpu.VMEM((NX,) + block, BF),
            dma((6,)),
            dma, dma((NZ,)), dma, dma, dma((NZ,)),
            dma, dma((NZ,)),
            dma, dma((NZ,)),
            dma, dma, dma, dma((2,)), dma, dma,
            dma, dma,
            dma, dma((UNITS + 1,)), dma((UNITS + 1,)),
            dma, dma, dma, dma,
        ],
        compiler_params=pltpu.CompilerParams(
            collective_id=0, has_side_effects=True, vmem_limit_bytes=40 * 1024 * 1024
        ),
        name="attend",
    )(*(pltpu.with_memory_space_constraint(a, pltpu.HBM) for a in (queries, keys, values, mask, out_proj.T)))


def solution(mesh):
    placed = (
        P("seq", "head"),
        P("head", "seq", None),
        P("head", "seq", None),
        P(None, "seq"),
        P("head", "seq"),
    )
    return jax.shard_map(
        on_device, mesh=mesh, in_specs=placed, out_specs=P("seq", "head"), check_vma=False
    )
```

time: 71.7 us -> 65.8 us (0.918)
  Pallas kernels: 70.1 us -> 65.1 us
    pallas_call x1, Pallas kernels: 70.1 us -> 65.1 us  [on_device(): pl.pallas_call(kernel, out_shape=jax.ShapeDtypeStruct(block, BF), in_spec...]
where the time goes in v3:
time: 65.8 us; the launch traced here: 65.7 us
  Pallas kernels  65.1 us (99%)
    pallas_call x1, Pallas kernels, on_device(): pl.pallas_call(kernel, out_shape=jax.ShapeDtypeStruct(block, BF), in_spec...  65.1 us

profile of v3, /device:TPU:1, one launch (start us, length us, event | category | flops | bytes accessed | tf_op | source)
XLA Modules:
  0.0 65.7 jit_solution(10432069459632555460)
XLA Ops:
  0.0 65.1 %attend.1 = bf16[16,512]{1,0:T(8,128)(2,1)S(1)} custom-call(bf16[16,512]{1,0:T(8,128)(2,1)} %q_hbm.1, bf16[1,2048,128]{2,1,0:T(8,128)(2,1)} %k_hbm.1, bf16[1,2048,128]{2,1,0:T(8,128)(2,1)} %v_hbm.1, s32[8,16]{1,0:T(8,128)} %mask_hbm.1, bf16[64,512]{1,0:T(8,128)(2,1)} %bitcast.1), custom_call_target="tpu_custom_call" | custom-call | tf_op jit(solution)/shard_map/attend/pallas_call | solution.py:405
  65.1 0.6 copy.7

commit v4 on v3

--- a/solution.py
+++ b/solution.py
@@ -37,9 +37,9 @@
 def kernel(
     q_hbm, k_hbm, v_hbm, mask_hbm, w_hbm, o_ref,
     m_buf, k2, v_buf, cm, q_buf, q2, p_send, y_recv, z_send, z_recv, n_recv, d_recv,
-    a_send, a_recv, w_buf, c_send, c_recv, o_send, o_recv,
+    a_send, a_recv, w_buf, w_other, o_send, o_recv,
     loc, qz_s, qz_r, qf_s, qb_s, qb_r, qy_s, qy_r, ps_s, ps_r, z_s, z_r, n_s, n_r, d_s, d_r,
-    a_s, a_r, w_s, wr_r, wl_r, c_s, c_r, o_s, o_r,
+    a_s, a_r, w_s, wr_r, wl_r, wc_s, wc_r, o_s, o_r,
 ):
     seq = lax.axis_index("seq")
     head = lax.axis_index("head")
@@ -98,7 +98,8 @@
     for d in range(1, NY):
         for offset in LAST:
             greet(at(ypeer(d), zmod(z - offset)), head)
-    greet(seq, partner)
+    for d in range(NY):
+        greet(at(ypeer(d), z), partner)
     for n in range(NX):
         @pl.when(jnp.logical_not(jnp.logical_and(own_out, x == n)))
         def _():
@@ -112,7 +113,7 @@
         for r in range(8):
             cm[r, :, b * BLK : (b + 1) * BLK] = jnp.broadcast_to(wide[r : r + 1], (8, BLK))
     q_load.wait()
-    pl.semaphore_wait(barrier, NY - 1 + len(NEAR) + len(LAST) * (NY - 1) + 1 + NX - own_out.astype(jnp.int32))
+    pl.semaphore_wait(barrier, NY - 1 + len(NEAR) + len(LAST) * (NY - 1) + NY + NX - own_out.astype(jnp.int32))
 
     def q_copy(b, send, d):
         ref = q_buf.at[b, y]
@@ -154,17 +155,28 @@
         ref = w_buf.at[zmod(z + i)]
         remote(ref, ref, w_s, wl_r.at[i + 1], left, head).start()
 
+    wide = NZ // 2
+
+    def w_share(b):
+        @pl.when(b // wide != core)
+        def _():
+            remote(w_buf.at[b], w_other.at[lax.rem(b, wide)], wc_s, wc_r, seq, partner).start()
+
     def w_relay(i):
         arrived(w_buf.at[zmod(z - i)], wr_r.at[i])
         if i < UNITS:
             w_ring_r(i)
+        w_share(zmod(z - i))
+        if i < UNITS:
             arrived(w_buf.at[zmod(z + i)], wl_r.at[i])
-        if i < UNITS - 1:
-            w_ring_l(i)
+            if i < UNITS - 1:
+                w_ring_l(i)
+            w_share(zmod(z + i))
 
     w_load.wait()
     w_ring_r(0)
     w_ring_l(0)
+    w_share(z)
 
     k_load.wait()
     k_again.wait()
@@ -340,6 +352,8 @@
     a_send[...] = total.astype(BF)
     for d in range(1, NY):
         remote(a_send, a_recv.at[d - 1], a_s, a_r, at(ypeer(d), z), head).start()
+        remote(a_send, a_recv.at[NY - 1 + d], a_s, a_r, at(ypeer(d), z), partner).start()
+    remote(a_send, a_recv.at[NY - 1], a_s, a_r, seq, partner).start()
 
     left_here(z_recv.at[:3], qz_s)
     left_here(z_recv.at[:6], qf_s)
@@ -352,20 +366,16 @@
     arrived(a_recv, a_r)
     w_relay(8)
 
-    rows = [a_send[...]] + [a_recv[d] for d in range(NY - 1)]
-    attended = jnp.concatenate(rows, axis=0)
-    wide = NZ // 2
-
-    def project(c):
-        columns = w_buf[pl.ds(c * wide, wide)].reshape(wide * w_buf.shape[1], w_buf.shape[2])
+    arrived(w_other, wc_r)
+
+    def project(rows, blocks):
+        columns = blocks.reshape(wide * w_buf.shape[1], w_buf.shape[2])
+        attended = jnp.concatenate(rows, axis=0)
         return lax.dot_general(attended, columns, (((1,), (1,)), ((), ())), preferred_element_type=F32)
 
-    c_send[...] = project(1 - core).astype(BF)
-    swap = remote(c_send, c_recv, c_s, c_r, seq, partner)
-    swap.start()
-    share = project(core)
-    swap.wait_recv()
-    o_send[...] = (share + c_recv[...].astype(F32)).astype(BF).reshape(o_send.shape)
+    share = project([a_send[...]] + [a_recv[d] for d in range(NY - 1)], w_buf[pl.ds(core * wide, wide)])
+    share = share + project([a_recv[NY - 1 + d] for d in range(NY)], w_other[...])
+    o_send[...] = share.astype(BF).reshape(o_send.shape)
     for d in range(NY):
         to = lax.rem(y - d + NY, NY)
         copy = remote(o_send.at[d], o_recv.at[x], o_s, o_r, at(to, z), 2 * y + core)
@@ -380,7 +390,7 @@
         else:
             copy.start()
 
-    swap.wait_send()
+    left_here(w_other, wc_s)
     left_here(a_recv, a_s)
     left_here(w_buf.at[: NZ - 1], w_s)
     arrived(o_recv, o_r)
@@ -421,10 +431,9 @@
             pltpu.VMEM((2, len(FAR)) + block, BF),
             pltpu.VMEM((len(LAST), NY) + block, BF),
             pltpu.VMEM(block, BF),
-            pltpu.VMEM((NY - 1,) + block, BF),
+            pltpu.VMEM((2 * NY - 1,) + block, BF),
             pltpu.VMEM((NZ,) + out_proj.shape[::-1], BF),
-            pltpu.VMEM((NY * ROWS, width), BF),
-            pltpu.VMEM((NY * ROWS, width), BF),
+            pltpu.VMEM((NZ // 2,) + out_proj.shape[::-1], BF),
             pltpu.VMEM((NY,) + block, BF),
             pltpu.VMEM((NX,) + block, BF),
             dma((6,)),

time: 65.8 us -> 65.7 us (level)
  no operation moved by 1% of the time
where the time goes in v4:
time: 65.7 us; the launch traced here: 65.6 us
  Pallas kernels  65 us (99%)
    pallas_call x1, Pallas kernels, on_device(): pl.pallas_call(kernel, out_shape=jax.ShapeDtypeStruct(block, BF), in_spec...  65 us

profile of v4, /device:TPU:1, one launch (start us, length us, event | category | flops | bytes accessed | tf_op | source)
XLA Modules:
  0.0 65.6 jit_solution(10328995128655928165)
XLA Ops:
  0.0 65.0 %attend.1 = bf16[16,512]{1,0:T(8,128)(2,1)S(1)} custom-call(bf16[16,512]{1,0:T(8,128)(2,1)} %q_hbm.1, bf16[1,2048,128]{2,1,0:T(8,128)(2,1)} %k_hbm.1, bf16[1,2048,128]{2,1,0:T(8,128)(2,1)} %v_hbm.1, s32[8,16]{1,0:T(8,128)} %mask_hbm.1, bf16[64,512]{1,0:T(8,128)(2,1)} %bitcast.1), custom_call_target="tpu_custom_call" | custom-call | tf_op jit(solution)/shard_map/attend/pallas_call | solution.py:415
  65.0 0.6 copy.7
